TPU v7x, 256 devices: a whole 4x4x8 slice. The times are simulated.
256 devices in a mesh: tile: 32 (over z, y_lo, core), freq: 8 (over y_hi, x).
Axes of the slice: x: 4, y: 4 (y_hi: 2, y_lo: 2; y = y_hi * 2 + y_lo), z: 8, core: 2. Of those that a mesh axis runs over, the one named last changes fastest.
Arguments:
- wavefield: bfloat16 [8, 2, 16384, 256], P('freq', None, 'tile'), may hold values from -6 to 6
- row_factors: bfloat16 [8, 2, 32768, 1024], P('freq', None, 'tile'), may hold values from -0.125 to 0.125
- col_factors: bfloat16 [8, 2, 16384, 2048], P('freq', None, 'tile'), may hold values from -0.1875 to 0.1875
- window_index: int32 [256], replicated, may hold values from 1 to 15
Outputs:
- adjoint_field: float32 [8, 2, 16384, 256], P('freq', None, 'tile')
All inputs are finite; a program needn't handle non-finite values.
Results may differ from a plain program's by a relative error of at most 0.0038.
Values may be sent and summed in bfloat16 or wider, within the bound.
A program may use at most 128 MiB of HBM per device.

v0:
```python
import functools
import math

import jax
import jax.numpy as jnp
import numpy as np
from jax import lax
from jax.experimental import pallas as pl
from jax.experimental.pallas import tpu as pltpu
from jax.sharding import PartitionSpec as P

TS = 512
RANK = 32
NT = 16
FREQS = 8
ZN = 8
XN = 4
VP = 256
LANES = 128
HALVES = 2
ROW_TILES = 2
SHARE = TS // FREQS
GROUP = 4 * ROW_TILES
MESH = pl.DeviceIdType.MESH
F32 = jnp.float32
BF16 = jnp.bfloat16


def transform_matrices():
    times, freqs = np.meshgrid(np.arange(NT), np.arange(FREQS), indexing="ij")
    angles = math.pi / NT * (2 * freqs + 1) * times
    eye = np.eye(16)
    forward = np.concatenate([np.kron(0.25 * np.cos(angles), eye), np.kron(-0.25 * np.sin(angles), eye)], 1)
    both = np.stack([forward, forward.T])
    high = both.astype(BF16)
    low = (both - high.astype(np.float64)).astype(BF16)
    return np.stack([high, low])


def zdelta(k):
    return jnp.where(k % 2 == 1, (k + 1) // 2, ZN - k // 2)


def dot(left, right):
    return jnp.dot(left, right, preferred_element_type=F32)


def dot_t(left, right):
    return lax.dot_general(left, right, (((0,), (0,)), ((), ())), preferred_element_type=F32)


def turned(pair, sign):
    re, im = pair[:, :LANES], pair[:, LANES:]
    return jnp.concatenate([-im, re] if sign > 0 else [im, -re], 1)


def kernel(
    wave_hbm, row_hbm, col_hbm, index_ref, mats_ref, out_ref,
    wave, row, col, x_one, x_two,
    c_send, c_recv, y_send, y_recv, f_send, f_recv, r_send, r_recv,
    load_wave, load_row, load_col,
    send_a, send_b, send_c, send_d, recv_a, recv_b, recv_c, recv_d,
):
    me, freq = lax.axis_index("tile"), lax.axis_index("freq")
    my_z, my_y, my_core = me // 4, (me // 2) % 2, me % 2

    loads = [
        pltpu.make_async_copy(wave_hbm.at[0], wave, load_wave),
        pltpu.make_async_copy(col_hbm.at[0], col, load_col),
        pltpu.make_async_copy(row_hbm.at[0], row, load_row),
    ]
    for load in loads:
        load.start()

    def tile_peer(k, q):
        z = (my_z + zdelta(k)) % ZN
        return z * 4 + ((my_y + q // 2) % 2) * 2 + (my_core + q % 2) % 2

    def freq_peer(n):
        return (freq + n) % FREQS

    barrier = pltpu.get_barrier_semaphore()
    for q in range(1, 4):
        pl.semaphore_signal(barrier, inc=1, device_id={"tile": tile_peer(0, q)}, device_id_type=MESH)

    def greet(k, carry):
        for q in range(4):
            pl.semaphore_signal(barrier, inc=1, device_id={"tile": tile_peer(k, q)}, device_id_type=MESH)
        return carry

    lax.fori_loop(1, ZN, greet, 0)
    for n in range(1, FREQS):
        pl.semaphore_signal(barrier, inc=1, device_id={"freq": freq_peer(n)}, device_id_type=MESH)

    loads[0].wait()
    for h in range(HALVES):
        xr = wave[0, :, h * LANES : (h + 1) * LANES]
        xi = wave[1, :, h * LANES : (h + 1) * LANES]
        x_one[:, 2 * h * LANES : (2 * h + 1) * LANES] = xr
        x_one[:, (2 * h + 1) * LANES : (2 * h + 2) * LANES] = xi
        x_two[:, 2 * h * LANES : (2 * h + 1) * LANES] = xi
        x_two[:, (2 * h + 1) * LANES : (2 * h + 2) * LANES] = -xr

    def copy_a(h, peer, k, q):
        return pltpu.make_async_remote_copy(
            src_ref=c_send.at[h, pl.ds(ROW_TILES * peer, ROW_TILES)],
            dst_ref=c_recv.at[h, :, me],
            send_sem=send_a.at[h, 4 * k + q],
            recv_sem=recv_a.at[h],
            device_id={"tile": peer},
            device_id_type=MESH,
        )

    def copy_d(h, peer, k, q):
        return pltpu.make_async_remote_copy(
            src_ref=r_send.at[h, :, peer],
            dst_ref=r_recv.at[h, pl.ds(ROW_TILES * me, ROW_TILES)],
            send_sem=send_d.at[h, 4 * k + q],
            recv_sem=recv_d.at[h, my_z],
            device_id={"tile": peer},
            device_id_type=MESH,
        )

    def own_a(h):
        return pltpu.make_async_copy(
            c_send.at[h, pl.ds(ROW_TILES * me, ROW_TILES)], c_recv.at[h, :, me], recv_a.at[h]
        )

    def own_d(h):
        return pltpu.make_async_copy(
            r_send.at[h, :, me], r_recv.at[h, pl.ds(ROW_TILES * me, ROW_TILES)], recv_d.at[h, my_z]
        )

    def copy_b(h, n):
        peer = freq_peer(n)
        return pltpu.make_async_remote_copy(
            src_ref=y_send.at[h, :, peer],
            dst_ref=y_recv.at[h, :, freq],
            send_sem=send_b.at[h, n],
            recv_sem=recv_b.at[h],
            device_id={"freq": peer},
            device_id_type=MESH,
        )

    def copy_c(h, n):
        peer = freq_peer(n)
        return pltpu.make_async_remote_copy(
            src_ref=f_send.at[h, :, peer],
            dst_ref=f_recv.at[h, :, freq],
            send_sem=send_c.at[h, n],
            recv_sem=recv_c.at[h],
            device_id={"freq": peer},
            device_id_type=MESH,
        )

    def groups(step, first=1):
        def body(k, carry):
            for q in range(4):
                step(k, q)
            return carry

        lax.fori_loop(first, ZN, body, 0)
        for q in range(1, 4):
            step(0, q)

    def project(k):
        z = (my_z + zdelta(k)) % ZN
        columns = pl.ds(pl.multiple_of(z * 256, 256), 256)
        value = dot_t(col[0, :, columns], x_one[...]) + dot_t(col[1, :, columns], x_two[...])
        value = value.astype(BF16)
        for h in range(HALVES):
            c_send[h, pl.ds(GROUP * z, GROUP)] = value[:, 256 * h : 256 * (h + 1)].reshape(GROUP, RANK, 256)

    loads[1].wait()
    with jax.named_scope("entry_barrier"):
        pl.semaphore_wait(barrier, 31 + 7)

    with jax.named_scope("coeffs_and_send"):

        def first(k, carry):
            project(k)
            for q in range(4):
                copy_a(0, tile_peer(k, q), k, q).start()
            return carry

        lax.fori_loop(1, ZN, first, 0)
        project(0)
        for q in range(1, 4):
            copy_a(0, tile_peer(0, q), 0, q).start()
        for h in range(HALVES):
            own_a(h).start()

    with jax.named_scope("second_coeffs_send"):

        def second(k, q):
            peer = tile_peer(k, q)
            copy_a(0, peer, k, q).wait_send()
            copy_a(1, peer, k, q).start()

        groups(second)

    loads[2].wait()

    def spectra(h):
        pltpu.make_async_copy(c_recv.at[h], c_recv.at[h], recv_a.at[h]).wait()
        for i in range(ROW_TILES):
            c_one = c_recv[h, i].reshape(32 * RANK, 256)
            rows = slice(i * TS, (i + 1) * TS)
            value = dot(row[0, rows], c_one) + dot(row[1, rows], turned(c_one, 1))
            y_send[h, i] = value.astype(BF16).reshape(FREQS, SHARE, 256)
        for n in range(1, FREQS):
            copy_b(h, n).start()
        pltpu.make_async_copy(y_send.at[h, :, freq], y_recv.at[h, :, freq], recv_b.at[h]).start()

    def window(h):
        pltpu.make_async_copy(y_recv.at[h], y_recv.at[h], recv_b.at[h]).wait()
        times = lax.broadcasted_iota(jnp.int32, (256, LANES), 0) // 16
        kept = times < index_ref[:, h * LANES : (h + 1) * LANES]
        kept = jnp.concatenate([kept.astype(F32)] * 2, 1) > 0.5
        for i in range(ROW_TILES):
            for b in range(2):
                blocks = []
                for u in range(2):
                    rows = slice((2 * b + u) * 16, (2 * b + u + 1) * 16)
                    block = y_recv[h, i, :, rows].reshape(FREQS * 16, 256)
                    blocks.append(jnp.concatenate([block[:, :LANES], block[:, LANES:]], 0))
                block = jnp.concatenate(blocks, 1)
                timed = dot(mats_ref[0, 0], block) + dot(mats_ref[1, 0], block)
                timed = jnp.where(kept, timed, 0.0)
                high = timed.astype(BF16)
                low = (timed - high.astype(F32)).astype(BF16)
                value = dot(mats_ref[0, 1], high) + (dot(mats_ref[1, 1], high) + dot(mats_ref[0, 1], low))
                value = value.astype(BF16)
                for u in range(2):
                    rows = slice((2 * b + u) * 16, (2 * b + u + 1) * 16)
                    part = value[:, u * LANES : (u + 1) * LANES]
                    f_send[h, i, :, rows] = jnp.concatenate([part[:128], part[128:]], 1).reshape(FREQS, 16, 256)
        for n in range(1, FREQS):
            copy_c(h, n).start()
        pltpu.make_async_copy(f_send.at[h, :, freq], f_recv.at[h, :, freq], recv_c.at[h]).start()

    def returned(h):
        pltpu.make_async_copy(f_recv.at[h], f_recv.at[h], recv_c.at[h]).wait()
        for i in range(ROW_TILES):
            f_one = f_recv[h, i].reshape(TS, 256)
            rows = slice(i * TS, (i + 1) * TS)
            value = dot_t(row[0, rows], f_one) + dot_t(row[1, rows], turned(f_one, -1))
            r_send[h, i] = value.astype(BF16).reshape(32, RANK, 256)

        def send(k, q):
            peer = tile_peer(k, q)
            (copy_a(1, peer, k, q) if h == 0 else copy_d(0, peer, k, q)).wait_send()
            copy_d(h, peer, k, q).start()

        groups(send)
        own_d(h).start()

    def adjoint(h):
        def step(z, first):
            held = r_recv.at[h, pl.ds(GROUP * z, GROUP)]
            pltpu.make_async_copy(held, held, recv_d.at[h, z]).wait()
            columns = pl.ds(pl.multiple_of(z * 256, 256), 256)
            r_one = held[...].reshape(256, 256)
            value = dot(col[0, :, columns], r_one) + dot(col[1, :, columns], turned(r_one, 1))
            for c in range(2):
                part = value[:, c * LANES : (c + 1) * LANES]
                old = out_ref[0, c, :, h * LANES : (h + 1) * LANES]
                out_ref[0, c, :, h * LANES : (h + 1) * LANES] = part if first else old + part

        step(my_z, True)

        def body(k, carry):
            step((my_z + zdelta(k)) % ZN, False)
            return carry

        lax.fori_loop(1, ZN, body, 0)

    for h in range(HALVES):
        with jax.named_scope("spectra%d" % h):
            spectra(h)
        with jax.named_scope("window%d" % h):
            window(h)
        with jax.named_scope("returned%d" % h):
            returned(h)
    for h in range(HALVES):
        with jax.named_scope("adjoint%d" % h):
            adjoint(h)

    with jax.named_scope("drain"):
        groups(lambda k, q: copy_d(1, tile_peer(k, q), k, q).wait_send())
        for h in range(HALVES):
            for n in range(1, FREQS):
                copy_b(h, n).wait_send()
                copy_c(h, n).wait_send()


def local(mats, wavefield, row_factors, col_factors, window_index):
    vmem = pl.BlockSpec(memory_space=pltpu.VMEM)
    hbm = pl.BlockSpec(memory_space=pl.ANY)
    dma = pltpu.SemaphoreType.DMA
    shape = wavefield.shape
    return pl.pallas_call(
        kernel,
        out_shape=jax.ShapeDtypeStruct(shape, F32),
        in_specs=[hbm, hbm, hbm, vmem, vmem],
        out_specs=vmem,
        scratch_shapes=[
            pltpu.VMEM((2, TS, VP), BF16),
            pltpu.VMEM((2, ROW_TILES * TS, 1024), BF16),
            pltpu.VMEM((2, TS, 2048), BF16),
            pltpu.VMEM((TS, 512), BF16),
            pltpu.VMEM((TS, 512), BF16),
            pltpu.VMEM((HALVES, 64, RANK, 256), BF16),
            pltpu.VMEM((HALVES, ROW_TILES, 32, RANK, 256), BF16),
            pltpu.VMEM((HALVES, ROW_TILES, FREQS, SHARE, 256), BF16),
            pltpu.VMEM((HALVES, ROW_TILES, FREQS, SHARE, 256), BF16),
            pltpu.VMEM((HALVES, ROW_TILES, FREQS, SHARE, 256), BF16),
            pltpu.VMEM((HALVES, ROW_TILES, FREQS, SHARE, 256), BF16),
            pltpu.VMEM((HALVES, ROW_TILES, 32, RANK, 256), BF16),
            pltpu.VMEM((HALVES, 64, RANK, 256), BF16),
            dma, dma, dma,
            dma((HALVES, 32)), dma((HALVES, FREQS)), dma((HALVES, FREQS)), dma((HALVES, 32)),
            dma((HALVES,)), dma((HALVES,)), dma((HALVES,)), dma((HALVES, ZN)),
        ],
        compiler_params=pltpu.CompilerParams(
            collective_id=0, has_side_effects=True, vmem_limit_bytes=56 << 20
        ),
        cost_estimate=pl.CostEstimate(flops=9_000_000_000, bytes_accessed=11_000_000, transcendentals=0),
    )(wavefield, row_factors, col_factors, window_index.reshape(1, VP), jnp.asarray(mats))


def solution(mesh):
    in_specs = (
        P("freq", None, "tile", None),
        P("freq", None, "tile", None),
        P("freq", None, "tile", None),
        P(),
    )
    return jax.shard_map(
        functools.partial(local, transform_matrices()),
        mesh=mesh,
        in_specs=in_specs,
        out_specs=P("freq", None, "tile", None),
        check_vma=False,
    )
```

profile of v0, /device:TPU:1, one launch (start us, length us, event | category | flops | bytes accessed | tf_op | source)
XLA Modules:
  0.0 125.4 jit_solution(14813799520359030107)
XLA Ops:
  0.0 123.1 %shard_map.55 = f32[1,2,512,256]{3,2,1,0:T(8,128)} custom-call(bf16[1,2,512,256]{3,2,1,0:T(8,128)(2,1)} %wave_hbm.1, bf16[1,2,1024,1024]{3,2,1,0:T(8,128)(2,1)} %row_hbm.1, bf16[1,2,512,2048]{3,2,1,0:T(8,128)(2,1)} %col_hbm.1, s32[1,256]{1,0:T(1,128)} %bitcast.1, bf16[2,2,256,256]{3,2,1,0:T(8,128)(2,1)} %constant.2.clone.mats_ref), custom_call_target="tpu_custom_call" | custom-call | flops 8999999488 | bytes 11000000 | tf_op jit(solution)/shard_map/pallas_call | solution.py:302
  123.1 2.3 %copy.7 = f32[1,2,512,256]{3,2,1,0:T(8,128)} copy(f32[1,2,512,256]{3,2,1,0:T(8,128)} %shard_map.55) | data formatting | bytes 2097152
where the time goes:
time: 127 us; the launch traced here: 125 us
  Pallas kernels  123 us (97%)
  local copies, waits for them, and re-layouts  2.26 us (2%)
    pallas_call x1, Pallas kernels, local(): pl.pallas_call(kernel, out_shape=jax.ShapeDtypeStruct(shape, F32), in_spe...  123 us

commit v1 on v0

v1 whole, which is shorter than its diff:
```python
import functools
import math

import jax
import jax.numpy as jnp
import numpy as np
from jax import lax
from jax.experimental import pallas as pl
from jax.experimental.pallas import tpu as pltpu
from jax.sharding import PartitionSpec as P

TS = 512
RANK = 32
NT = 16
FREQS = 8
ZN = 8
XN = 4
VP = 256
LANES = 128
HALVES = 2
ROW_TILES = 2
SHARE = TS // FREQS
GROUP = 4 * ROW_TILES
CHUNKS = [(h, i) for h in range(HALVES) for i in range(ROW_TILES)]
MESH = pl.DeviceIdType.MESH
F32 = jnp.float32
BF16 = jnp.bfloat16


def transform_matrices():
    times, freqs = np.meshgrid(np.arange(NT), np.arange(FREQS), indexing="ij")
    angles = math.pi / NT * (2 * freqs + 1) * times
    eye = np.eye(16)
    forward = np.concatenate([np.kron(0.25 * np.cos(angles), eye), np.kron(-0.25 * np.sin(angles), eye)], 1)
    both = np.stack([forward, forward.T])
    high = both.astype(BF16)
    low = (both - high.astype(np.float64)).astype(BF16)
    return np.stack([high, low])


def zdelta(k):
    return jnp.where(k % 2 == 1, (k + 1) // 2, ZN - k // 2)


def dot(left, right):
    return jnp.dot(left, right, preferred_element_type=F32)


def dot_t(left, right):
    return lax.dot_general(left, right, (((0,), (0,)), ((), ())), preferred_element_type=F32)


def turned(pair, sign):
    re, im = pair[:, :LANES], pair[:, LANES:]
    return jnp.concatenate([-im, re] if sign > 0 else [im, -re], 1)


def kernel(
    wave_hbm, row_hbm, col_hbm, index_ref, mats_ref, out_ref,
    wave, row, col, x_one, x_two,
    c_send, c_recv, y_send, y_recv, f_send, f_recv, r_send, r_recv,
    load_wave, load_row, load_col,
    send_a, send_b, send_c, send_d, recv_a, recv_b, recv_c, recv_d,
):
    me, freq = lax.axis_index("tile"), lax.axis_index("freq")
    my_z, my_y, my_core = me // 4, (me // 2) % 2, me % 2

    def col_load(k):
        z = (my_z + zdelta(k)) % ZN
        columns = pl.ds(pl.multiple_of(z * 256, 256), 256)
        return pltpu.make_async_copy(col_hbm.at[0, :, :, columns], col.at[:, :, columns], load_col.at[k])

    wave_load = pltpu.make_async_copy(wave_hbm.at[0], wave, load_wave)
    row_load = pltpu.make_async_copy(row_hbm.at[0], row, load_row)
    wave_load.start()
    for k in range(1, ZN):
        col_load(k).start()
    col_load(0).start()

    def tile_peer(k, q):
        z = (my_z + zdelta(k)) % ZN
        return z * 4 + ((my_y + q // 2) % 2) * 2 + (my_core + q % 2) % 2

    def freq_peer(n):
        return (freq + n) % FREQS

    barrier = pltpu.get_barrier_semaphore()
    for q in range(1, 4):
        pl.semaphore_signal(barrier, inc=1, device_id={"tile": tile_peer(0, q)}, device_id_type=MESH)

    def greet(k, carry):
        for q in range(4):
            pl.semaphore_signal(barrier, inc=1, device_id={"tile": tile_peer(k, q)}, device_id_type=MESH)
        return carry

    lax.fori_loop(1, ZN, greet, 0)
    for n in range(1, FREQS):
        pl.semaphore_signal(barrier, inc=1, device_id={"freq": freq_peer(n)}, device_id_type=MESH)

    wave_load.wait()
    for h in range(HALVES):
        xr = wave[0, :, h * LANES : (h + 1) * LANES]
        xi = wave[1, :, h * LANES : (h + 1) * LANES]
        x_one[:, 2 * h * LANES : (2 * h + 1) * LANES] = xr
        x_one[:, (2 * h + 1) * LANES : (2 * h + 2) * LANES] = xi
        x_two[:, 2 * h * LANES : (2 * h + 1) * LANES] = xi
        x_two[:, (2 * h + 1) * LANES : (2 * h + 2) * LANES] = -xr

    def copy_a(h, i, peer, k, q):
        return pltpu.make_async_remote_copy(
            src_ref=c_send.at[h, ROW_TILES * peer + i],
            dst_ref=c_recv.at[h, i, me],
            send_sem=send_a.at[h, i],
            recv_sem=recv_a.at[h, i],
            device_id={"tile": peer},
            device_id_type=MESH,
        )

    def copy_d(h, i, peer, k, q):
        return pltpu.make_async_remote_copy(
            src_ref=r_send.at[h, i, peer],
            dst_ref=r_recv.at[h, ROW_TILES * me + i],
            send_sem=send_d.at[h, i],
            recv_sem=recv_d.at[h, my_z],
            device_id={"tile": peer},
            device_id_type=MESH,
        )

    def own_a(h, i):
        return pltpu.make_async_copy(c_send.at[h, ROW_TILES * me + i], c_recv.at[h, i, me], recv_a.at[h, i])

    def own_d(h, i):
        return pltpu.make_async_copy(r_send.at[h, i, me], r_recv.at[h, ROW_TILES * me + i], recv_d.at[h, my_z])

    def copy_b(h, i, n):
        peer = freq_peer(n)
        return pltpu.make_async_remote_copy(
            src_ref=y_send.at[h, i, peer],
            dst_ref=y_recv.at[h, i, freq],
            send_sem=send_b.at[h, i],
            recv_sem=recv_b.at[h, i],
            device_id={"freq": peer},
            device_id_type=MESH,
        )

    def copy_c(h, i, n):
        peer = freq_peer(n)
        return pltpu.make_async_remote_copy(
            src_ref=f_send.at[h, i, peer],
            dst_ref=f_recv.at[h, i, freq],
            send_sem=send_c.at[h, i],
            recv_sem=recv_c.at[h, i],
            device_id={"freq": peer},
            device_id_type=MESH,
        )

    def groups(step, first=1):
        def body(k, carry):
            for q in range(4):
                step(k, q)
            return carry

        lax.fori_loop(first, ZN, body, 0)
        for q in range(1, 4):
            step(0, q)

    def project(k):
        z = (my_z + zdelta(k)) % ZN
        columns = pl.ds(pl.multiple_of(z * 256, 256), 256)
        value = dot_t(col[0, :, columns], x_one[...]) + dot_t(col[1, :, columns], x_two[...])
        value = value.astype(BF16)
        for h in range(HALVES):
            c_send[h, pl.ds(GROUP * z, GROUP)] = value[:, 256 * h : 256 * (h + 1)].reshape(GROUP, RANK, 256)

    with jax.named_scope("coeffs_and_send"):

        def send_first(k):
            for q in range(4):
                copy_a(0, 0, tile_peer(k, q), k, q).start()

        col_load(1).wait()
        project(1)
        pl.semaphore_wait(barrier, 31 + 7)
        send_first(1)

        def first(k, carry):
            col_load(k).wait()
            project(k)
            send_first(k)
            return carry

        lax.fori_loop(2, ZN, first, 0)
        col_load(0).wait()
        project(0)
        for q in range(1, 4):
            copy_a(0, 0, tile_peer(0, q), 0, q).start()
        row_load.start()

    with jax.named_scope("later_coeffs_send"):
        own_a(0, 0).start()
        for h, i in CHUNKS[1:]:
            groups(lambda k, q: copy_a(h, i, tile_peer(k, q), k, q).start())
            own_a(h, i).start()

    def spectra(h, i):
        if (h, i) == (0, 0):
            row_load.wait()
        pltpu.make_async_copy(c_recv.at[h, i], c_recv.at[h, i], recv_a.at[h, i]).wait()
        c_one = c_recv[h, i].reshape(32 * RANK, 256)
        rows = slice(i * TS, (i + 1) * TS)
        value = dot(row[0, rows], c_one) + dot(row[1, rows], turned(c_one, 1))
        y_send[h, i] = value.astype(BF16).reshape(FREQS, SHARE, 256)
        for n in range(1, FREQS):
            copy_b(h, i, n).start()
        pltpu.make_async_copy(y_send.at[h, i, freq], y_recv.at[h, i, freq], recv_b.at[h, i]).start()

    def window(h, i):
        pltpu.make_async_copy(y_recv.at[h, i], y_recv.at[h, i], recv_b.at[h, i]).wait()
        times = lax.broadcasted_iota(jnp.int32, (256, LANES), 0) // 16
        kept = times < index_ref[:, h * LANES : (h + 1) * LANES]
        kept = jnp.concatenate([kept.astype(F32)] * 2, 1) > 0.5
        for b in range(2):
            blocks = []
            for u in range(2):
                rows = slice((2 * b + u) * 16, (2 * b + u + 1) * 16)
                block = y_recv[h, i, :, rows].reshape(FREQS * 16, 256)
                blocks.append(jnp.concatenate([block[:, :LANES], block[:, LANES:]], 0))
            block = jnp.concatenate(blocks, 1)
            timed = dot(mats_ref[0, 0], block) + dot(mats_ref[1, 0], block)
            timed = jnp.where(kept, timed, 0.0)
            high = timed.astype(BF16)
            low = (timed - high.astype(F32)).astype(BF16)
            value = dot(mats_ref[0, 1], high) + (dot(mats_ref[1, 1], high) + dot(mats_ref[0, 1], low))
            value = value.astype(BF16)
            for u in range(2):
                rows = slice((2 * b + u) * 16, (2 * b + u + 1) * 16)
                part = value[:, u * LANES : (u + 1) * LANES]
                f_send[h, i, :, rows] = jnp.concatenate([part[:128], part[128:]], 1).reshape(FREQS, 16, 256)
        for n in range(1, FREQS):
            copy_c(h, i, n).start()
        pltpu.make_async_copy(f_send.at[h, i, freq], f_recv.at[h, i, freq], recv_c.at[h, i]).start()

    def returned(h, i):
        pltpu.make_async_copy(f_recv.at[h, i], f_recv.at[h, i], recv_c.at[h, i]).wait()
        f_one = f_recv[h, i].reshape(TS, 256)
        rows = slice(i * TS, (i + 1) * TS)
        value = dot_t(row[0, rows], f_one) + dot_t(row[1, rows], turned(f_one, -1))
        r_send[h, i] = value.astype(BF16).reshape(32, RANK, 256)
        groups(lambda k, q: copy_d(h, i, tile_peer(k, q), k, q).start())
        own_d(h, i).start()

    def adjoint(h):
        def step(z, first):
            held = r_recv.at[h, pl.ds(GROUP * z, GROUP)]
            pltpu.make_async_copy(held, held, recv_d.at[h, z]).wait()
            columns = pl.ds(pl.multiple_of(z * 256, 256), 256)
            r_one = held[...].reshape(256, 256)
            value = dot(col[0, :, columns], r_one) + dot(col[1, :, columns], turned(r_one, 1))
            for c in range(2):
                part = value[:, c * LANES : (c + 1) * LANES]
                old = out_ref[0, c, :, h * LANES : (h + 1) * LANES]
                out_ref[0, c, :, h * LANES : (h + 1) * LANES] = part if first else old + part

        step(my_z, True)

        def body(k, carry):
            step((my_z + zdelta(k)) % ZN, False)
            return carry

        lax.fori_loop(1, ZN, body, 0)

    for step in range(len(CHUNKS) + 2):
        for lag, stage in enumerate((spectra, window, returned)):
            if 0 <= step - lag < len(CHUNKS):
                stage(*CHUNKS[step - lag])
    for h in range(HALVES):
        adjoint(h)

    with jax.named_scope("drain"):
        for h, i in CHUNKS:
            sent = r_send.at[h, i, pl.ds(0, 31)]
            pltpu.make_async_copy(sent, sent, send_a.at[h, i]).wait()
            pltpu.make_async_copy(sent, sent, send_d.at[h, i]).wait()
            sent = y_send.at[h, i, pl.ds(0, FREQS - 1)]
            pltpu.make_async_copy(sent, sent, send_b.at[h, i]).wait()
            pltpu.make_async_copy(sent, sent, send_c.at[h, i]).wait()


def local(mats, wavefield, row_factors, col_factors, window_index):
    vmem = pl.BlockSpec(memory_space=pltpu.VMEM)
    hbm = pl.BlockSpec(memory_space=pl.ANY)
    dma = pltpu.SemaphoreType.DMA
    shape = wavefield.shape
    return pl.pallas_call(
        kernel,
        out_shape=pltpu.VMEM(shape, F32),
        in_specs=[hbm, hbm, hbm, vmem, vmem],
        out_specs=vmem,
        scratch_shapes=[
            pltpu.VMEM((2, TS, VP), BF16),
            pltpu.VMEM((2, ROW_TILES * TS, 1024), BF16),
            pltpu.VMEM((2, TS, 2048), BF16),
            pltpu.VMEM((TS, 512), BF16),
            pltpu.VMEM((TS, 512), BF16),
            pltpu.VMEM((HALVES, 64, RANK, 256), BF16),
            pltpu.VMEM((HALVES, ROW_TILES, 32, RANK, 256), BF16),
            pltpu.VMEM((HALVES, ROW_TILES, FREQS, SHARE, 256), BF16),
            pltpu.VMEM((HALVES, ROW_TILES, FREQS, SHARE, 256), BF16),
            pltpu.VMEM((HALVES, ROW_TILES, FREQS, SHARE, 256), BF16),
            pltpu.VMEM((HALVES, ROW_TILES, FREQS, SHARE, 256), BF16),
            pltpu.VMEM((HALVES, ROW_TILES, 32, RANK, 256), BF16),
            pltpu.VMEM((HALVES, 64, RANK, 256), BF16),
            dma, dma, dma((ZN,)),
            *[dma((HALVES, ROW_TILES))] * 4,
            *[dma((HALVES, ROW_TILES))] * 3, dma((HALVES, ZN)),
        ],
        compiler_params=pltpu.CompilerParams(
            collective_id=0, has_side_effects=True, vmem_limit_bytes=56 << 20
        ),
        cost_estimate=pl.CostEstimate(flops=9_000_000_000, bytes_accessed=11_000_000, transcendentals=0),
    )(wavefield, row_factors, col_factors, window_index.reshape(1, VP), jnp.asarray(mats))


def solution(mesh):
    in_specs = (
        P("freq", None, "tile", None),
        P("freq", None, "tile", None),
        P("freq", None, "tile", None),
        P(),
    )
    return jax.shard_map(
        functools.partial(local, transform_matrices()),
        mesh=mesh,
        in_specs=in_specs,
        out_specs=P("freq", None, "tile", None),
        check_vma=False,
    )
```

time: 127 us -> 108 us (0.85); the launches traced: 125 us -> 108 us
  Pallas kernels: 123 us -> 107 us
  local copies, waits for them, and re-layouts: 2.26 us -> 0.97 us
    pallas_call x1, Pallas kernels: 123 us -> 107 us  [local(): pl.pallas_call(kernel, out_shape=pltpu.VMEM(shape, F32), in_specs=[hbm, h...]
    unnamed x1, local copies, waits for them, and re-layouts: 2.26 us -> 0.97 us
where the time goes in v1:
time: 108 us
  Pallas kernels  107 us (99%)
    pallas_call x1, Pallas kernels, local(): pl.pallas_call(kernel, out_shape=pltpu.VMEM(shape, F32), in_specs=[hbm, h...  107 us

profile of v1, /device:TPU:1, one launch (start us, length us, event | category | flops | bytes accessed | tf_op | source)
XLA Modules:
  0.0 108.2 jit_solution(8969080109099586795)
XLA Ops:
  0.0 107.2 %shard_map.55 = f32[1,2,512,256]{3,2,1,0:T(8,128)S(1)} custom-call(bf16[1,2,512,256]{3,2,1,0:T(8,128)(2,1)} %wave_hbm.1, bf16[1,2,1024,1024]{3,2,1,0:T(8,128)(2,1)} %row_hbm.1, bf16[1,2,512,2048]{3,2,1,0:T(8,128)(2,1)} %col_hbm.1, s32[1,256]{1,0:T(1,128)} %bitcast.1, bf16[2,2,256,256]{3,2,1,0:T(8,128)(2,1)} %constant.2.clone.mats_ref), custom_call_target="tpu_custom_call" | custom-call | flops 8999999488 | bytes 11000000 | tf_op jit(solution)/shard_map/pallas_call | solution.py:294
  107.2 1.0 copy.7

commit v2 on v1

--- a/solution.py
+++ b/solution.py
@@ -56,10 +56,10 @@
 
 
 def kernel(
-    wave_hbm, row_hbm, col_hbm, index_ref, mats_ref, out_ref,
-    wave, row, col, x_one, x_two,
+    wave_hbm, row_hbm, col_hbm, index_hbm, mats_hbm, out_ref,
+    wave, row, col, index_ref, mats_ref, x_one, x_two,
     c_send, c_recv, y_send, y_recv, f_send, f_recv, r_send, r_recv,
-    load_wave, load_row, load_col,
+    load_wave, load_row, load_col, load_index, load_mats,
     send_a, send_b, send_c, send_d, recv_a, recv_b, recv_c, recv_d,
 ):
     me, freq = lax.axis_index("tile"), lax.axis_index("freq")
@@ -72,10 +72,10 @@
 
     wave_load = pltpu.make_async_copy(wave_hbm.at[0], wave, load_wave)
     row_load = pltpu.make_async_copy(row_hbm.at[0], row, load_row)
+    index_load = pltpu.make_async_copy(index_hbm, index_ref, load_index)
+    mats_load = pltpu.make_async_copy(mats_hbm, mats_ref, load_mats)
     wave_load.start()
-    for k in range(1, ZN):
-        col_load(k).start()
-    col_load(0).start()
+    col_load(1).start()
 
     def tile_peer(k, q):
         z = (my_z + zdelta(k)) % ZN
@@ -85,17 +85,20 @@
         return (freq + n) % FREQS
 
     barrier = pltpu.get_barrier_semaphore()
+    def greet(k, carry):
+        for q in range(4):
+            pl.semaphore_signal(barrier, inc=1, device_id={"tile": tile_peer(ZN - k, q)}, device_id_type=MESH)
+        return carry
+
+    lax.fori_loop(1, ZN, greet, 0)
     for q in range(1, 4):
         pl.semaphore_signal(barrier, inc=1, device_id={"tile": tile_peer(0, q)}, device_id_type=MESH)
-
-    def greet(k, carry):
-        for q in range(4):
-            pl.semaphore_signal(barrier, inc=1, device_id={"tile": tile_peer(k, q)}, device_id_type=MESH)
-        return carry
-
-    lax.fori_loop(1, ZN, greet, 0)
     for n in range(1, FREQS):
         pl.semaphore_signal(barrier, inc=1, device_id={"freq": freq_peer(n)}, device_id_type=MESH)
+
+    for k in range(2, ZN):
+        col_load(k).start()
+    col_load(0).start()
 
     wave_load.wait()
     for h in range(HALVES):
@@ -154,15 +157,16 @@
             device_id_type=MESH,
         )
 
-    def groups(step, first=1):
+    def groups(step):
+        for q in range(1, 4):
+            step(0, q)
+
         def body(k, carry):
             for q in range(4):
                 step(k, q)
             return carry
 
-        lax.fori_loop(first, ZN, body, 0)
-        for q in range(1, 4):
-            step(0, q)
+        lax.fori_loop(1, ZN, body, 0)
 
     def project(k):
         z = (my_z + zdelta(k)) % ZN
@@ -195,6 +199,8 @@
         for q in range(1, 4):
             copy_a(0, 0, tile_peer(0, q), 0, q).start()
         row_load.start()
+        index_load.start()
+        mats_load.start()
 
     with jax.named_scope("later_coeffs_send"):
         own_a(0, 0).start()
@@ -215,6 +221,9 @@
         pltpu.make_async_copy(y_send.at[h, i, freq], y_recv.at[h, i, freq], recv_b.at[h, i]).start()
 
     def window(h, i):
+        if (h, i) == (0, 0):
+            index_load.wait()
+            mats_load.wait()
         pltpu.make_async_copy(y_recv.at[h, i], y_recv.at[h, i], recv_b.at[h, i]).wait()
         times = lax.broadcasted_iota(jnp.int32, (256, LANES), 0) // 16
         kept = times < index_ref[:, h * LANES : (h + 1) * LANES]
@@ -270,7 +279,7 @@
         lax.fori_loop(1, ZN, body, 0)
 
     for step in range(len(CHUNKS) + 2):
-        for lag, stage in enumerate((spectra, window, returned)):
+        for lag, stage in ((2, returned), (1, window), (0, spectra)):
             if 0 <= step - lag < len(CHUNKS):
                 stage(*CHUNKS[step - lag])
     for h in range(HALVES):
@@ -294,12 +303,14 @@
     return pl.pallas_call(
         kernel,
         out_shape=pltpu.VMEM(shape, F32),
-        in_specs=[hbm, hbm, hbm, vmem, vmem],
+        in_specs=[hbm] * 5,
         out_specs=vmem,
         scratch_shapes=[
             pltpu.VMEM((2, TS, VP), BF16),
             pltpu.VMEM((2, ROW_TILES * TS, 1024), BF16),
             pltpu.VMEM((2, TS, 2048), BF16),
+            pltpu.VMEM((1, VP), jnp.int32),
+            pltpu.VMEM((2, 2, 256, 256), BF16),
             pltpu.VMEM((TS, 512), BF16),
             pltpu.VMEM((TS, 512), BF16),
             pltpu.VMEM((HALVES, 64, RANK, 256), BF16),
@@ -310,7 +321,7 @@
             pltpu.VMEM((HALVES, ROW_TILES, FREQS, SHARE, 256), BF16),
             pltpu.VMEM((HALVES, ROW_TILES, 32, RANK, 256), BF16),
             pltpu.VMEM((HALVES, 64, RANK, 256), BF16),
-            dma, dma, dma((ZN,)),
+            dma, dma, dma((ZN,)), dma, dma,
             *[dma((HALVES, ROW_TILES))] * 4,
             *[dma((HALVES, ROW_TILES))] * 3, dma((HALVES, ZN)),
         ],

time: 108 us -> 106 us (0.981)
  Pallas kernels: 107 us -> 105 us
    pallas_call x1, Pallas kernels: 107 us -> 105 us  [local(): pl.pallas_call(kernel, out_shape=pltpu.VMEM(shape, F32), in_specs=[hbm] *...]
where the time goes in v2:
time: 106 us
  Pallas kernels  105 us (99%)
    pallas_call x1, Pallas kernels, local(): pl.pallas_call(kernel, out_shape=pltpu.VMEM(shape, F32), in_specs=[hbm] *...  105 us

profile of v2, /device:TPU:1, one launch (start us, length us, event | category | flops | bytes accessed | tf_op | source)
XLA Modules:
  0.0 105.7 jit_solution(18270744296746154151)
XLA Ops:
  0.0 104.7 %shard_map.55 = f32[1,2,512,256]{3,2,1,0:T(8,128)S(1)} custom-call(bf16[1,2,512,256]{3,2,1,0:T(8,128)(2,1)} %wave_hbm.1, bf16[1,2,1024,1024]{3,2,1,0:T(8,128)(2,1)} %row_hbm.1, bf16[1,2,512,2048]{3,2,1,0:T(8,128)(2,1)} %col_hbm.1, s32[1,256]{1,0:T(1,128)} %bitcast.1, bf16[2,2,256,256]{3,2,1,0:T(8,128)(2,1)} %constant.2.clone.mats_hbm), custom_call_target="tpu_custom_call" | custom-call | flops 8999999488 | bytes 11000000 | tf_op jit(solution)/shard_map/pallas_call | solution.py:303
  104.7 1.0 copy.7

commit v3 on v2

--- a/solution.py
+++ b/solution.py
@@ -113,7 +113,7 @@
         return pltpu.make_async_remote_copy(
             src_ref=c_send.at[h, ROW_TILES * peer + i],
             dst_ref=c_recv.at[h, i, me],
-            send_sem=send_a.at[h, i],
+            send_sem=send_a,
             recv_sem=recv_a.at[h, i],
             device_id={"tile": peer},
             device_id_type=MESH,
@@ -123,8 +123,8 @@
         return pltpu.make_async_remote_copy(
             src_ref=r_send.at[h, i, peer],
             dst_ref=r_recv.at[h, ROW_TILES * me + i],
-            send_sem=send_d.at[h, i],
-            recv_sem=recv_d.at[h, my_z],
+            send_sem=send_d,
+            recv_sem=recv_d.at[my_z if h else ZN],
             device_id={"tile": peer},
             device_id_type=MESH,
         )
@@ -133,14 +133,14 @@
         return pltpu.make_async_copy(c_send.at[h, ROW_TILES * me + i], c_recv.at[h, i, me], recv_a.at[h, i])
 
     def own_d(h, i):
-        return pltpu.make_async_copy(r_send.at[h, i, me], r_recv.at[h, ROW_TILES * me + i], recv_d.at[h, my_z])
+        return pltpu.make_async_copy(r_send.at[h, i, me], r_recv.at[h, ROW_TILES * me + i], recv_d.at[my_z if h else ZN])
 
     def copy_b(h, i, n):
         peer = freq_peer(n)
         return pltpu.make_async_remote_copy(
             src_ref=y_send.at[h, i, peer],
             dst_ref=y_recv.at[h, i, freq],
-            send_sem=send_b.at[h, i],
+            send_sem=send_b,
             recv_sem=recv_b.at[h, i],
             device_id={"freq": peer},
             device_id_type=MESH,
@@ -151,7 +151,7 @@
         return pltpu.make_async_remote_copy(
             src_ref=f_send.at[h, i, peer],
             dst_ref=f_recv.at[h, i, freq],
-            send_sem=send_c.at[h, i],
+            send_sem=send_c,
             recv_sem=recv_c.at[h, i],
             device_id={"freq": peer},
             device_id_type=MESH,
@@ -261,7 +261,8 @@
     def adjoint(h):
         def step(z, first):
             held = r_recv.at[h, pl.ds(GROUP * z, GROUP)]
-            pltpu.make_async_copy(held, held, recv_d.at[h, z]).wait()
+            if h == 1:
+                pltpu.make_async_copy(held, held, recv_d.at[z]).wait()
             columns = pl.ds(pl.multiple_of(z * 256, 256), 256)
             r_one = held[...].reshape(256, 256)
             value = dot(col[0, :, columns], r_one) + dot(col[1, :, columns], turned(r_one, 1))
@@ -270,6 +271,8 @@
                 old = out_ref[0, c, :, h * LANES : (h + 1) * LANES]
                 out_ref[0, c, :, h * LANES : (h + 1) * LANES] = part if first else old + part
 
+        if h == 0:
+            pltpu.make_async_copy(r_recv.at[0], r_recv.at[0], recv_d.at[ZN]).wait()
         step(my_z, True)
 
         def body(k, carry):
@@ -282,17 +285,15 @@
         for lag, stage in ((2, returned), (1, window), (0, spectra)):
             if 0 <= step - lag < len(CHUNKS):
                 stage(*CHUNKS[step - lag])
-    for h in range(HALVES):
-        adjoint(h)
-
-    with jax.named_scope("drain"):
-        for h, i in CHUNKS:
-            sent = r_send.at[h, i, pl.ds(0, 31)]
-            pltpu.make_async_copy(sent, sent, send_a.at[h, i]).wait()
-            pltpu.make_async_copy(sent, sent, send_d.at[h, i]).wait()
-            sent = y_send.at[h, i, pl.ds(0, FREQS - 1)]
-            pltpu.make_async_copy(sent, sent, send_b.at[h, i]).wait()
-            pltpu.make_async_copy(sent, sent, send_c.at[h, i]).wait()
+    adjoint(0)
+    sent = c_send.at[:, pl.ds(0, 62)]
+    pltpu.make_async_copy(sent, sent, send_a).wait()
+    for sem in (send_b, send_c):
+        sent = y_send.at[:, :, pl.ds(0, FREQS - 1)]
+        pltpu.make_async_copy(sent, sent, sem).wait()
+    adjoint(1)
+    sent = r_send.at[:, :, pl.ds(0, 31)]
+    pltpu.make_async_copy(sent, sent, send_d).wait()
 
 
 def local(mats, wavefield, row_factors, col_factors, window_index):
@@ -322,8 +323,8 @@
             pltpu.VMEM((HALVES, ROW_TILES, 32, RANK, 256), BF16),
             pltpu.VMEM((HALVES, 64, RANK, 256), BF16),
             dma, dma, dma((ZN,)), dma, dma,
-            *[dma((HALVES, ROW_TILES))] * 4,
-            *[dma((HALVES, ROW_TILES))] * 3, dma((HALVES, ZN)),
+            dma, dma, dma, dma,
+            *[dma((HALVES, ROW_TILES))] * 3, dma((ZN + 1,)),
         ],
         compiler_params=pltpu.CompilerParams(
             collective_id=0, has_side_effects=True, vmem_limit_bytes=56 << 20

time: 106 us -> 106 us (level)
  no operation moved by 1% of the time
where the time goes in v3:
time: 106 us
  Pallas kernels  105 us (99%)
    pallas_call x1, Pallas kernels, local(): pl.pallas_call(kernel, out_shape=pltpu.VMEM(shape, F32), in_specs=[hbm] *...  105 us

profile of v3, /device:TPU:1, one launch (start us, length us, event | category | flops | bytes accessed | tf_op | source)
XLA Modules:
  0.0 105.5 jit_solution(2067639308058364320)
XLA Ops:
  0.0 104.5 %shard_map.55 = f32[1,2,512,256]{3,2,1,0:T(8,128)S(1)} custom-call(bf16[1,2,512,256]{3,2,1,0:T(8,128)(2,1)} %wave_hbm.1, bf16[1,2,1024,1024]{3,2,1,0:T(8,128)(2,1)} %row_hbm.1, bf16[1,2,512,2048]{3,2,1,0:T(8,128)(2,1)} %col_hbm.1, s32[1,256]{1,0:T(1,128)} %bitcast.1, bf16[2,2,256,256]{3,2,1,0:T(8,128)(2,1)} %constant.2.clone.mats_hbm), custom_call_target="tpu_custom_call" | custom-call | flops 8999999488 | bytes 11000000 | tf_op jit(solution)/shard_map/pallas_call | solution.py:304
  104.5 1.0 copy.7

commit v4 on v3

--- a/solution.py
+++ b/solution.py
@@ -158,15 +158,15 @@
         )
 
     def groups(step):
-        for q in range(1, 4):
-            step(0, q)
-
         def body(k, carry):
             for q in range(4):
                 step(k, q)
             return carry
 
-        lax.fori_loop(1, ZN, body, 0)
+        lax.fori_loop(1, 5, body, 0)
+        for q in range(1, 4):
+            step(0, q)
+        lax.fori_loop(5, ZN, body, 0)
 
     def project(k):
         z = (my_z + zdelta(k)) % ZN
@@ -259,27 +259,39 @@
         own_d(h, i).start()
 
     def adjoint(h):
-        def step(z, first):
+        def product(z):
             held = r_recv.at[h, pl.ds(GROUP * z, GROUP)]
-            if h == 1:
-                pltpu.make_async_copy(held, held, recv_d.at[z]).wait()
             columns = pl.ds(pl.multiple_of(z * 256, 256), 256)
             r_one = held[...].reshape(256, 256)
-            value = dot(col[0, :, columns], r_one) + dot(col[1, :, columns], turned(r_one, 1))
+            return dot(col[0, :, columns], r_one) + dot(col[1, :, columns], turned(r_one, 1))
+
+        def arrived(z):
+            if h == 1:
+                held = r_recv.at[h, pl.ds(GROUP * z, GROUP)]
+                pltpu.make_async_copy(held, held, recv_d.at[z]).wait()
+
+        def add(zs, first=False):
+            for z in zs:
+                arrived(z)
+            value = functools.reduce(lambda a, b: a + b, [product(z) for z in zs])
             for c in range(2):
                 part = value[:, c * LANES : (c + 1) * LANES]
                 old = out_ref[0, c, :, h * LANES : (h + 1) * LANES]
                 out_ref[0, c, :, h * LANES : (h + 1) * LANES] = part if first else old + part
 
+        def place(k):
+            return (my_z + zdelta(k)) % ZN
+
         if h == 0:
             pltpu.make_async_copy(r_recv.at[0], r_recv.at[0], recv_d.at[ZN]).wait()
-        step(my_z, True)
+        add([my_z], True)
 
         def body(k, carry):
-            step((my_z + zdelta(k)) % ZN, False)
+            add([place(k)])
             return carry
 
-        lax.fori_loop(1, ZN, body, 0)
+        lax.fori_loop(1, 6, body, 0)
+        add([place(k) for k in range(6, ZN)])
 
     for step in range(len(CHUNKS) + 2):
         for lag, stage in ((2, returned), (1, window), (0, spectra)):

time: 106 us -> 106 us (level)
  no operation moved by 1% of the time
where the time goes in v4:
time: 106 us
  Pallas kernels  105 us (99%)
    pallas_call x1, Pallas kernels, local(): pl.pallas_call(kernel, out_shape=pltpu.VMEM(shape, F32), in_specs=[hbm] *...  105 us

profile of v4, /device:TPU:1, one launch (start us, length us, event | category | flops | bytes accessed | tf_op | source)
XLA Modules:
  0.0 105.9 jit_solution(4096348998019803324)
XLA Ops:
  0.0 105.0 %shard_map.55 = f32[1,2,512,256]{3,2,1,0:T(8,128)S(1)} custom-call(bf16[1,2,512,256]{3,2,1,0:T(8,128)(2,1)} %wave_hbm.1, bf16[1,2,1024,1024]{3,2,1,0:T(8,128)(2,1)} %row_hbm.1, bf16[1,2,512,2048]{3,2,1,0:T(8,128)(2,1)} %col_hbm.1, s32[1,256]{1,0:T(1,128)} %bitcast.1, bf16[2,2,256,256]{3,2,1,0:T(8,128)(2,1)} %constant.2.clone.mats_hbm), custom_call_target="tpu_custom_call" | custom-call | flops 8999999488 | bytes 11000000 | tf_op jit(solution)/shard_map/pallas_call | solution.py:316
  105.0 1.0 copy.7
